TPU v7x, 768 devices: a whole 4x8x12 slice. The times are simulated.
768 devices in a mesh: inter: 32 (over x, z_hi, core), intra: 24 (over z_lo, y).
Axes of the slice: x: 4, y: 8, z: 12 (z_hi: 4, z_lo: 3; z = z_hi * 3 + z_lo), core: 2. Of those that a mesh axis runs over, the one named last changes fastest.
Arguments:
- tokens: bfloat16 [4608, 8192], P('intra'), may hold values from -6 to 6
- weight_codes: bfloat16 [14592, 8192], P(('inter', 'intra')), may hold values from -6 to 6
- exponents: int32 [14592, 64], P(('inter', 'intra')), may hold values from -8 to -6
- upstream: bfloat16 [4608, 14592], P('intra', 'inter'), may hold values from -6 to 6
Outputs:
- activation: bfloat16 [4608, 14592], P('intra', 'inter')
- grad_input: float32 [4608, 8192], P('intra', 'inter')
All inputs are finite; a program needn't handle non-finite values.
Results may differ from a plain program's by a relative error of at most 0.018.
Values may be sent and summed in bfloat16 or wider, within the bound.
A program may use at most 64 MiB of HBM per device.

v0:
```python
import jax
import jax.numpy as jnp
from jax import lax
from jax.sharding import PartitionSpec as P


def expand(weight_codes, exponents):
    row_count, row_width = weight_codes.shape
    block_scale = jnp.exp2(exponents.astype(jnp.float32)).astype(jnp.bfloat16)
    blocks = weight_codes.reshape(row_count, row_width // 128, 128) * block_scale[:, :, None]
    return blocks.reshape(row_count, row_width)


def block_forward(tokens, upstream, weights):
    projected = lax.dot_general(
        tokens, weights, (((1,), (1,)), ((), ())), preferred_element_type=jnp.float32
    )
    sig_value = jax.nn.sigmoid(projected)
    activation = (projected * sig_value).astype(jnp.bfloat16)
    columns = upstream.astype(jnp.float32)
    grad_hidden = (columns * sig_value * (1.0 + projected * (1.0 - sig_value))).astype(jnp.bfloat16)
    return (activation, grad_hidden)


def per_device(tokens, weight_codes, exponents, upstream):
    gathered = lax.all_gather(expand(weight_codes, exponents), "intra", axis=0, tiled=True)
    activation, grad_hidden = block_forward(tokens, upstream, gathered)
    result = (activation, jnp.dot(grad_hidden, gathered, preferred_element_type=jnp.float32))
    activation = result[0]
    grad_input = lax.psum_scatter(
        result[1].astype(jnp.bfloat16), "inter", scatter_dimension=1, tiled=True
    ).astype(jnp.float32)
    return (activation, grad_input)


def solution(mesh):
    placed = (
        P("intra", None),
        P(("inter", "intra"), None),
        P(("inter", "intra"), None),
        P("intra", "inter"),
    )
    return jax.shard_map(
        per_device,
        mesh=mesh,
        in_specs=placed,
        out_specs=(P("intra", "inter"), P("intra", "inter")),
        check_vma=False,
    )
```

profile of v0, /device:TPU:1, one launch (start us, length us, event | category | flops | bytes accessed | tf_op | source)
XLA Modules:
  0.0 304.3 jit_solution(12301182867979648635)
XLA Ops:
  7.2 0.0 copy-start
  7.2 0.0 all-gather.3.cloned.1.call-start
  7.2 0.9 exponential_convert_fusion
  8.1 0.2 mul.23
  8.4 0.3 copy.6
  8.6 1.8 multiply_bitcast_fusion
  10.4 0.0 all-gather.3.cloned.1.call-update
  10.5 0.0 reduce-scatter.2.cloned.1.call-start
  10.5 127.9 %all-gather.3.cloned.1.call-done = bf16[24,19,8192]{2,1,0:T(8,128)(2,1)} async-done(((bf16[1,19,8192]{2,1,0:T(8,128)(2,1)}), bf16[24,19,8192]{2,1,0:T(8,128)(2,1)}) %all-gather.3.cloned.1.call-update) | async-done | bytes 7471120 | tf_op jit(solution)/shard_map/all_gather | solution.py:26
  138.5 9.0 %reshape.9 = bf16[456,8192]{1,0:T(8,128)(2,1)} reshape(bf16[24,19,8192]{2,1,0:T(8,128)(2,1)} %all-gather.3.cloned.1.call-done) | data formatting | bytes 14942208
  147.4 0.0 copy-done
  147.4 0.0 copy-start.1
  147.4 0.0 copy-start.2
  147.4 6.3 %multiply_convert_fusion.1 = (bf16[192,456]{1,0:T(8,128)(2,1)}, f32[192,456]{1,0:T(8,128)S(1)}) fusion(bf16[456,8192]{1,0:T(8,128)(2,1)} %reshape.9, bf16[192,8192]{1,0:T(8,128)(2,1)S(1)} %copy-done), kind=kOutput, calls=%fused_computation.3 | convolution fusion | flops 1434889728 | bytes 11142144 | tf_op jit(solution)/shard_map/dot_general | solution.py:15
  153.7 0.0 copy-done.1
  153.7 0.0 copy-done.2
  153.7 3.8 %convolution_convert_fusion = bf16[192,8192]{1,0:T(8,128)(2,1)} fusion(bf16[456,8192]{1,0:T(8,128)(2,1)S(1)} %copy-done.1, f32[192,456]{1,0:T(8,128)S(1)} %get-tuple-element.3, bf16[192,456]{1,0:T(8,128)(2,1)S(1)} %copy-done.2), kind=kOutput, calls=%fused_computation | convolution fusion | flops 1436900352 | bytes 11142144 | tf_op jit(solution)/shard_map/dot_general | solution.py:28
  157.5 0.0 reduce-scatter.2.cloned.1.call-update
  157.5 138.4 %reduce-scatter.2.cloned.1.call-done = bf16[192,256]{1,0:T(8,128)(2,1)} async-done(((bf16[192,8192]{1,0:T(8,128)(2,1)}), bf16[192,256]{1,0:T(8,128)(2,1)}) %reduce-scatter.2.cloned.1.call-update) | async-done | bytes 98320 | tf_op jit(solution)/shard_map/reduce_scatter | solution.py:30
  295.9 1.6 convert_element_type.27
  (1 shorter events, 0.0 us)
Async XLA Ops:
  7.2 140.3 %copy-start = (bf16[192,8192]{1,0:T(8,128)(2,1)S(1)}, bf16[192,8192]{1,0:T(8,128)(2,1)}, u32[]{:S(2)}) copy-start(bf16[192,8192]{1,0:T(8,128)(2,1)} %param.4) | copy-start | bytes 9437188
  7.2 131.3 %all-gather.3.cloned.1.call-start = ((), (), s32[]{:S(2)}) async-start(), calls=%async_computation.2 | async-start | bytes 9830400 | tf_op jit(solution)/shard_map/all_gather | solution.py:26
  10.5 285.4 %reduce-scatter.2.cloned.1.call-start = ((), (), s32[]{:S(2)}) async-start(), calls=%async_computation.1 | async-start | bytes 3244032 | tf_op jit(solution)/shard_map/reduce_scatter | solution.py:30
  147.4 6.3 %copy-start.1 = (bf16[456,8192]{1,0:T(8,128)(2,1)S(1)}, bf16[456,8192]{1,0:T(8,128)(2,1)}, u32[]{:S(2)}) copy-start(bf16[456,8192]{1,0:T(8,128)(2,1)} %reshape.9) | copy-start | bytes 22413316
  147.4 6.3 %copy-start.2 = (bf16[192,456]{1,0:T(8,128)(2,1)S(1)}, bf16[192,456]{1,0:T(8,128)(2,1)}, u32[]{:S(2)}) copy-start(bf16[192,456]{1,0:T(8,128)(2,1)} %param.7) | copy-start | bytes 525316
Sparse Core Ops, SparseCore 0:
  10.6 127.8 all-gather.2
  157.6 138.1 reduce-scatter.1
where the time goes:
time: 305 us; the launch traced here: 304 us
  waiting for transfers between devices  266 us (87%)
  between operations  14.1 us (5%)
  matrix products  10 us (3%)
  local copies, waits for them, and re-layouts  9.5 us (3%)
  other arithmetic  4.26 us (1%)
    reduce_scatter x1, waiting for transfers between devices, per_device(): lax.psum_scatter(result[1].astype(jnp.bfloat16), 'inter', scatter_dimensi...  138 us
    all_gather x1, waiting for transfers between devices, per_device(): lax.all_gather(expand(weight_codes, exponents), 'intra', axis=0, tiled=True)  128 us
    unnamed x9, local copies, waits for them, and re-layouts  9.27 us
    dot_general x1, matrix products, block_forward(): lax.dot_general(tokens, weights, (((1,), (1,)), ((), ())), preferred_elem...  6.26 us
  transfers between devices with their start and end apart: 2, of which 2 were waited for; matrix products, arithmetic and copies ran while one was open for 0% of the time, Pallas kernels for 0%

commit v1 on v0

v1 whole, which is shorter than its diff:
```python
import jax
import jax.numpy as jnp
from jax import lax
from jax.experimental import pallas as pl
from jax.experimental.pallas import tpu as pltpu
from jax.sharding import PartitionSpec as P

MESH = pl.DeviceIdType.MESH
F32 = jnp.float32
BF16 = jnp.bfloat16

WINDOW = 768
WIDTH = 4 * WINDOW
ROWS = 192
SLOT = 64
NT = (((1,), (1,)), ((), ()))


def slot_of(offset):
    if offset == 0:
        return 0
    return 2 * offset - 1 if offset > 0 else -2 * offset


def device(x, y, z, core):
    x, y, z, core = lax.rem(x + 8, 4), lax.rem(y + 8, 8), lax.rem(z + 24, 12), lax.rem(core + 2, 2)
    return {"inter": x * 8 + (z // 3) * 2 + core, "intra": lax.rem(z, 3) * 8 + y}


def kernel(
    tokens, codes, exponents, upstream, act_out, grad_out,
    windows, remnants, gathered, tok, perm, up_perm, p_send, p_own, p_recv, act_perm, hidden,
    g_send, g_recv, g_own, x_send, x_mid, x_recv, z_send, z_recv,
    tok_own_sem, a2a_s, a2a_r, ring_s, ring_r, tok_s, tok_r, tokc_s, tokc_r,
    p_s, p_r, h_s, h_r, g_s, g_r, m_s, m_r, x_s, x_r, f_s, f_r,
):
    inter = lax.axis_index("inter")
    intra = lax.axis_index("intra")
    x, z_hi, core = inter // 8, lax.rem(inter // 2, 4), lax.rem(inter, 2)
    j, y = intra // 8, lax.rem(intra, 8)
    z = z_hi * 3 + j
    other_core = device(x, y, z, core + 1)

    def part(m):
        return lax.rem(j + m, 3)

    def group_peer(m):
        return {"inter": inter, "intra": part(m) * 8 + y}

    def rows_of(s, size=ROWS, start=0):
        return pl.ds(pl.multiple_of(s * ROWS + start, 16), size)

    def remote(src, dst, send_sem, recv_sem, to):
        return pltpu.make_async_remote_copy(
            src_ref=src, dst_ref=dst, send_sem=send_sem, recv_sem=recv_sem,
            device_id=to, device_id_type=MESH,
        )

    pending = []

    barrier = pltpu.get_barrier_semaphore()
    peers = [device(x, y, z + dz, core + dc) for dz in range(12) for dc in range(2) if dz or dc]
    peers += [device(x, y + 1, z, core), device(x, y + 7, z, core)]
    peers += [device(x + 1, y, z, core), device(x + 3, y, z, core)]
    for peer in peers:
        pl.semaphore_signal(barrier, inc=1, device_id=peer, device_id_type=MESH)

    def token_columns(q, to_part):
        return pl.ds(pl.multiple_of(q * 2048 + to_part * 640, 128), WINDOW)

    own_copies = [
        pltpu.make_async_copy(
            tokens.at[:, token_columns(q, j)],
            tok.at[rows_of(j), pl.ds(q * WINDOW, WINDOW)],
            tok_own_sem.at[q],
        )
        for q in range(4)
    ]
    for copy in own_copies:
        copy.start()

    scale = jnp.exp2(exponents[...].astype(F32)).astype(BF16).astype(F32)
    row = lax.broadcasted_iota(jnp.int32, (16, 128), 0)
    blank = jnp.zeros((32, 128), BF16)
    for q in range(4):
        for i in range(16):
            b = q * 16 + i
            value = codes[:, b * 128:(b + 1) * 128].astype(F32) * scale[:, b:b + 1]
            tail = jnp.zeros((16, 128), F32)
            for k in range(3):
                tail = jnp.where(row == 3 * j + k, value[16 + k:17 + k, :], tail)
            to = min(i // 5, 2)
            at = q * WINDOW + (i - 5 * to) * 128
            windows[to, 0:16, at:at + 128] = value[0:16].astype(BF16)
            windows[to, 16:32, at:at + 128] = tail.astype(BF16)
        for to in range(2):
            windows[to, :, q * WINDOW + 640:(q + 1) * WINDOW] = blank
    mine = pl.ds(pl.multiple_of(16 * j, 16), 16)
    gathered[mine, :] = windows[j, 0:16, :]

    pl.semaphore_wait(barrier, len(peers))

    a2a_main, a2a_tail = [], []
    for m in (1, 2):
        a2a_main.append(remote(
            windows.at[part(m), pl.ds(0, 16)], gathered.at[mine],
            a2a_s.at[0, m - 1], a2a_r.at[0, m - 1], group_peer(m)))
        a2a_tail.append(remote(
            windows.at[part(m), pl.ds(16, 16)], remnants.at[m - 1],
            a2a_s.at[1, m - 1], a2a_r.at[1, m - 1], group_peer(m)))
    for copy in a2a_main:
        copy.start()

    def unit_rows(u, offset):
        if u == 3:
            return pl.ds(slot_of(offset) * SLOT + 48, 16)
        return pl.ds(pl.multiple_of(slot_of(offset) * SLOT + 16 * part(u), 16), 16)

    def ring(u, way, k):
        sign = 1 if way == 0 else -1
        to = 4 if k == 4 else sign * k
        return remote(
            gathered.at[unit_rows(u, sign * (k - 1))], gathered.at[unit_rows(u, to)],
            ring_s.at[u, way, k - 1], ring_r.at[u, way, k - 1], device(x, y + sign, z, core))

    def goes(u, way, k):
        return k <= 3 or (k == 4 and u % 2 == way)

    def ring_start(u, way, k):
        if goes(u, way, k):
            copy = ring(u, way, k)
            copy.start()
            pending.append(copy)

    def ring_arrive(u, k):
        for way in (0, 1):
            if goes(u, way, k):
                ring(u, way, k).wait_recv()
                ring_start(u, way, k + 1)

    def ring_open(u):
        ring_start(u, 0, 1)
        ring_start(u, 1, 1)

    ring_open(0)
    for copy in a2a_tail:
        copy.start()
    pending += a2a_main + a2a_tail

    at = lax.broadcasted_iota(jnp.int32, (512, 456), 0)
    natural = lax.broadcasted_iota(jnp.int32, (512, 456), 1)
    slot, within = at >> 6, at & 63
    offset = jnp.where((slot & 1) == 1, (slot + 1) >> 1, -(slot >> 1))
    source_y = (y - offset + 8) & 7
    late = within - 48
    late_z = (late >= 3).astype(jnp.int32) + (late >= 6).astype(jnp.int32)
    source_z = jnp.where(late < 0, within >> 4, late_z)
    source_row = jnp.where(late < 0, within & 15, 16 + late - 3 * late_z)
    matches = (natural == (source_z * 8 + source_y) * 19 + source_row) & (late < 9)
    perm[...] = jnp.where(matches, 1.0, 0.0).astype(BF16)
    up_perm[...] = lax.dot_general(upstream[...], perm[...], NT, preferred_element_type=F32)

    token_copies = []
    for way, step, to_part in ((0, 1, part(1)), (1, 11, part(2))):
        for q in range(4):
            token_copies.append(remote(
                tokens.at[pl.ds(pl.multiple_of(96 * core, 16), 96), token_columns(q, to_part)],
                tok.at[rows_of(j, 96, 96 * core), pl.ds(q * WINDOW, WINDOW)],
                tok_s.at[way, q], tok_r.at[way, q], device(x, y, z + step, core)))

    ring_arrive(0, 1)
    for u in (1, 2):
        a2a_main[2 - u].wait_recv()
        ring_open(u)
    for copy in token_copies:
        copy.start()
    pending += token_copies
    ring_arrive(0, 2)
    for copy in a2a_tail:
        copy.wait_recv()
    gathered[48:64, :] = (
        windows[j, 16:32, :].astype(F32) + remnants[0].astype(F32) + remnants[1].astype(F32)
    ).astype(BF16)
    ring_open(3)
    ring_arrive(1, 1)
    ring_arrive(2, 1)
    ring_arrive(0, 3)
    ring_arrive(3, 1)
    ring_arrive(1, 2)
    ring_arrive(2, 2)
    ring_arrive(0, 4)
    ring_arrive(3, 2)

    core_copies = []
    for way in (0, 1):
        for q in range(4):
            token_copies[way * 4 + q].wait_recv()
        block = tok.at[rows_of(part(2 - way), 96, 96 * core)]
        copy = remote(block, block, tokc_s.at[way], tokc_r.at[way], other_core)
        copy.start()
        core_copies.append(copy)
    pending += core_copies

    ring_arrive(1, 3)
    ring_arrive(2, 3)
    ring_arrive(3, 3)
    for copy in core_copies:
        copy.wait_recv()
    for copy in own_copies:
        copy.wait()

    p_copies, h_copies = {}, {}

    def project(c):
        columns = pl.ds(c * 128, 128)
        for s in range(3):
            value = lax.dot_general(
                tok[s * ROWS:(s + 1) * ROWS, :], gathered[c * 128:(c + 1) * 128, :], NT,
                preferred_element_type=F32)
            p_send[s * ROWS:(s + 1) * ROWS, columns] = value.astype(BF16)

            @pl.when(j == s)
            def _():
                p_own[:, columns] = value

        for m in (1, 2):
            copy = remote(
                p_send.at[rows_of(part(m)), columns], p_recv.at[m - 1, :, columns],
                p_s.at[c, m - 1], p_r.at[c, m - 1], group_peer(m))
            copy.start()
            p_copies[c, m] = copy
            pending.append(copy)

    def activate(c):
        columns = pl.ds(c * 128, 128)
        for m in (1, 2):
            p_copies[c, m].wait_recv()
        projected = p_own[:, columns] + p_recv[0, :, columns].astype(F32) + p_recv[1, :, columns].astype(F32)
        sig = 1.0 / (1.0 + jnp.exp(-projected))
        act_perm[:, columns] = (projected * sig).astype(BF16)
        slope = sig * (1.0 + projected * (1.0 - sig))
        hidden[rows_of(j), columns] = (up_perm[:, columns] * slope).astype(BF16)
        for m in (1, 2):
            block = hidden.at[rows_of(j), columns]
            copy = remote(block, block, h_s.at[c, m - 1], h_r.at[c, m - 1], group_peer(m))
            copy.start()
            h_copies[c, m] = copy
            pending.append(copy)

    project(0)
    project(1)
    project(2)
    activate(0)
    activate(1)
    ring_arrive(1, 4)
    ring_arrive(2, 4)
    ring_arrive(3, 4)
    project(3)
    activate(2)
    activate(3)
    act_out[...] = jnp.dot(act_perm[...], perm[...], preferred_element_type=F32).astype(BF16)
    for c in range(4):
        for m in (1, 2):
            h_copies[c, m].wait_recv()

    g_copies = []

    def half(s, q, which):
        columns = pl.ds(pl.multiple_of(q * WINDOW + 384 * which, 128), 384)
        return jnp.dot(
            hidden[s * ROWS:(s + 1) * ROWS, :], gathered[:, columns], preferred_element_type=F32)

    for s in range(3):
        for q in range(4):
            g_send[s, q] = half(s, q, 1 - core).astype(BF16)
        copy = remote(g_send.at[s], g_recv.at[s], g_s.at[s], g_r.at[s], other_core)
        copy.start()
        g_copies.append(copy)
    pending += g_copies

    right, left = device(x + 1, y, z, core), device(x + 3, y, z, core)
    far, near, back = lax.rem(x + 2, 4), lax.rem(x + 1, 4), lax.rem(x + 3, 4)
    mid_copies, x_copies = {}, {}
    for s in range(3):
        for q in range(4):
            g_own[s, q] = half(s, q, core)
        g_copies[s].wait_recv()
        for q in range(4):
            g_own[s, q] = g_own[s, q] + g_recv[s, q].astype(F32)
        x_send[s, 0] = g_own[s, far].astype(BF16)
        for way, to in ((0, right), (1, left)):
            copy = remote(
                x_send.at[s, 0, pl.ds(96 * way, 96)], x_mid.at[s, way],
                m_s.at[s, way], m_r.at[s, way], to)
            copy.start()
            mid_copies[s, way] = copy
            pending.append(copy)
    for s in range(3):
        for way, to, quarter in ((0, right, near), (1, left, back)):
            mid_copies[s, way].wait_recv()
            own, there = pl.ds(96 * way, 96), pl.ds(96 - 96 * way, 96)
            x_send[s, 1 + way, own, :] = (g_own[s, quarter, own, :] + x_mid[s, way].astype(F32)).astype(BF16)
            x_send[s, 1 + way, there, :] = g_own[s, quarter, there, :].astype(BF16)
            copy = remote(x_send.at[s, 1 + way], x_recv.at[s, way], x_s.at[s, way], x_r.at[s, way], to)
            copy.start()
            x_copies[s, way] = copy
            pending.append(copy)

    last = []
    for s in range(3):
        for way in (0, 1):
            x_copies[s, way].wait_recv()
        z_send[s] = (g_own[s, x] + x_recv[s, 0].astype(F32) + x_recv[s, 1].astype(F32)).astype(BF16)
        for i in range(3):
            block = 5 * j + 3 * core + i
            owner, side = block // 2, lax.rem(block, 2)
            valid = jnp.logical_or(core == 0, j == 2) if i == 2 else True
            here = jnp.logical_and(owner == z_hi * 2 + core, j == s)
            src = z_send.at[s, :, pl.ds(128 * i, 128)]
            dst = z_recv.at[z_hi, :, pl.ds(pl.multiple_of(128 * side, 128), 128)]
            away = remote(
                src, dst, f_s.at[s, i], f_r.at[z_hi, side],
                {"inter": x * 8 + owner, "intra": s * 8 + y})
            stay = pltpu.make_async_copy(src, dst, f_r.at[z_hi, side])
            leaves = jnp.logical_and(valid, jnp.logical_not(here))

            @pl.when(leaves)
            def _():
                away.start()

            @pl.when(jnp.logical_and(valid, here))
            def _():
                stay.start()

            last.append((leaves, away))

    for copy in pending:
        copy.wait_send()
    for leaves, copy in last:
        @pl.when(leaves)
        def _():
            copy.wait_send()

    for source in range(4):
        for side in range(2):
            piece = z_recv.at[source, :, pl.ds(128 * side, 128)]
            pltpu.make_async_copy(piece, piece, f_r.at[source, side]).wait()
    grad_out[...] = (
        (z_recv[0].astype(F32) + z_recv[1].astype(F32)) + (z_recv[2].astype(F32) + z_recv[3].astype(F32))
    )


def per_device(tokens, weight_codes, exponents, upstream):
    vmem = pl.BlockSpec(memory_space=pltpu.VMEM)
    dma = pltpu.SemaphoreType.DMA
    return pl.pallas_call(
        kernel,
        out_shape=(
            jax.ShapeDtypeStruct((ROWS, 456), BF16),
            jax.ShapeDtypeStruct((ROWS, 256), F32),
        ),
        in_specs=[pl.BlockSpec(memory_space=pl.ANY), vmem, vmem, vmem],
        out_specs=(vmem, vmem),
        scratch_shapes=[
            pltpu.VMEM((3, 32, WIDTH), BF16),
            pltpu.VMEM((2, 16, WIDTH), BF16),
            pltpu.VMEM((512, WIDTH), BF16),
            pltpu.VMEM((3 * ROWS, WIDTH), BF16),
            pltpu.VMEM((512, 456), BF16),
            pltpu.VMEM((ROWS, 512), F32),
            pltpu.VMEM((3 * ROWS, 512), BF16),
            pltpu.VMEM((ROWS, 512), F32),
            pltpu.VMEM((2, ROWS, 512), BF16),
            pltpu.VMEM((ROWS, 512), BF16),
            pltpu.VMEM((3 * ROWS, 512), BF16),
            pltpu.VMEM((3, 4, ROWS, 384), BF16),
            pltpu.VMEM((3, 4, ROWS, 384), BF16),
            pltpu.VMEM((3, 4, ROWS, 384), F32),
            pltpu.VMEM((3, 3, ROWS, 384), BF16),
            pltpu.VMEM((3, 2, 96, 384), BF16),
            pltpu.VMEM((3, 2, ROWS, 384), BF16),
            pltpu.VMEM((3, ROWS, 384), BF16),
            pltpu.VMEM((4, ROWS, 256), BF16),
            dma((4,)),
            dma((2, 2)), dma((2, 2)),
            dma((4, 2, 4)), dma((4, 2, 4)),
            dma((2, 4)), dma((2, 4)),
            dma((2,)), dma((2,)),
            dma((4, 2)), dma((4, 2)),
            dma((4, 2)), dma((4, 2)),
            dma((3,)), dma((3,)),
            dma((3, 2)), dma((3, 2)),
            dma((3, 2)), dma((3, 2)),
            dma((3, 3)), dma((4, 2)),
        ],
        compiler_params=pltpu.CompilerParams(
            collective_id=0, has_side_effects=True, vmem_limit_bytes=48 << 20),
        cost_estimate=pl.CostEstimate(
            flops=4 * ROWS * 8192 * 456, bytes_accessed=8 << 20, transcendentals=ROWS * 512),
    )(tokens, weight_codes, exponents, upstream)


def solution(mesh):
    placed = (
        P("intra", None),
        P(("inter", "intra"), None),
        P(("inter", "intra"), None),
        P("intra", "inter"),
    )
    return jax.shard_map(
        per_device,
        mesh=mesh,
        in_specs=placed,
        out_specs=(P("intra", "inter"), P("intra", "inter")),
        check_vma=False,
    )
```

time: 305 us -> 112 us (0.37)
  the two profiles are of different devices: /device:TPU:1 before, /device:TPU:129 now
where the time goes in v1:
time: 112 us
  Pallas kernels  105 us (94%)
  local copies, waits for them, and re-layouts  5.87 us (5%)
    pallas_call x1, Pallas kernels, per_device(): pl.pallas_call(kernel, out_shape=(jax.ShapeDtypeStruct((ROWS, 456), BF16)...  105 us
    unnamed x10, local copies, waits for them, and re-layouts  5.87 us

profile of v1, /device:TPU:129, one launch (start us, length us, event | category | flops | bytes accessed | tf_op | source)
XLA Modules:
  0.0 111.7 jit_solution(10009287946559980049)
XLA Ops:
  0.6 0.0 copy-start
  0.6 1.9 %copy-done = bf16[192,8192]{1,0:T(8,128)(2,1)S(1)} copy-done((bf16[192,8192]{1,0:T(8,128)(2,1)S(1)}, bf16[192,8192]{1,0:T(8,128)(2,1)}, u32[]{:S(2)}) %copy-start) | copy-done | bytes 3145752
  2.5 0.0 copy-start.1
  2.5 1.0 copy-done.1
  3.5 0.0 copy-start.2
  3.5 0.9 copy-done.2
  4.4 0.0 copy-start.3
  4.4 0.7 copy-done.3
  5.2 105.2 %shard_map.59 = (bf16[192,456]{1,0:T(8,128)(2,1)S(1)}, f32[192,256]{1,0:T(8,128)S(1)}) custom-call(bf16[192,8192]{1,0:T(8,128)(2,1)S(1)} %copy-done, bf16[19,8192]{1,0:T(8,128)(2,1)S(1)} %copy-done.1, s32[19,64]{1,0:T(8,128)S(1)} %copy-done.3, bf16[192,456]{1,0:T(8,128)(2,1)S(1)} %copy-done.2), custom_call_target="tpu_custom_call" | custom-call | flops 2868903936 | bytes 8388608 | tf_op jit(solution)/shard_map/pallas_call | solution.py:356
  110.3 0.7 copy.8
  111.0 0.7 copy.9
Async XLA Ops:
  0.6 1.9 %copy-start = (bf16[192,8192]{1,0:T(8,128)(2,1)S(1)}, bf16[192,8192]{1,0:T(8,128)(2,1)}, u32[]{:S(2)}) copy-start(bf16[192,8192]{1,0:T(8,128)(2,1)} %tokens.1) | copy-start | bytes 9437188
  2.5 1.0 copy-start.1
  3.5 0.9 copy-start.2
  4.4 0.7 copy-start.3

commit v2 on v1

v2 whole, which is shorter than its diff:
```python
import jax
import jax.numpy as jnp
from jax import lax
from jax.experimental import pallas as pl
from jax.experimental.pallas import tpu as pltpu
from jax.sharding import PartitionSpec as P

MESH = pl.DeviceIdType.MESH
F32 = jnp.float32
BF16 = jnp.bfloat16

WINDOW = 768
WIDTH = 4 * WINDOW
ROWS = 192
SLOT = 64
PACK = 640
UNIT = WIDTH + PACK
PIECE = 96
CHUNKS = ((0, 256), (256, 128), (384, 128))
NT = (((1,), (1,)), ((), ()))


def slot_of(offset):
    if offset == 0:
        return 0
    return 2 * offset - 1 if offset > 0 else -2 * offset


def device(x, y, z, core):
    x, y, z, core = lax.rem(x + 8, 4), lax.rem(y + 8, 8), lax.rem(z + 24, 12), lax.rem(core + 2, 2)
    return {"inter": x * 8 + (z // 3) * 2 + core, "intra": lax.rem(z, 3) * 8 + y}


def kernel(
    tokens, codes_hbm, exponents_hbm, upstream_hbm, act_out, grad_out,
    codes, exponents, upstream,
    windows, packed, gathered, tok, perm, up_perm, p_part, p_send, p_recv, act_perm, hidden,
    g_send, g_recv, g_own, x_far, x_send, x_mid, x_recv, z_send, z_recv,
    load_sem, tok_own_sem, a2a_s, a2a_r, ring_s, ring_r, tok_s, tok_r, tokc_s, tokc_r,
    p_s, p_r, h_s, h_r, g_s, g_r, m_s, m_r, n_s, n_r, x_s, x_r, f_s, f_r,
):
    inter = lax.axis_index("inter")
    intra = lax.axis_index("intra")
    x, z_hi, core = inter // 8, lax.rem(inter // 2, 4), lax.rem(inter, 2)
    j, y = intra // 8, lax.rem(intra, 8)
    z = z_hi * 3 + j
    other_core = device(x, y, z, core + 1)

    def part(m):
        return lax.rem(j + m, 3)

    def group_peer(m):
        return {"inter": inter, "intra": part(m) * 8 + y}

    def rows_of(s, size=ROWS, start=0):
        return pl.ds(pl.multiple_of(s * ROWS + start, 16), size)

    def remote(src, dst, send_sem, recv_sem, to):
        return pltpu.make_async_remote_copy(
            src_ref=src, dst_ref=dst, send_sem=send_sem, recv_sem=recv_sem,
            device_id=to, device_id_type=MESH,
        )

    pending = []

    def launch(copy):
        copy.start()
        pending.append(copy)
        return copy

    barrier = pltpu.get_barrier_semaphore()
    peers = [device(x, y, z + dz, core + dc) for dz in range(12) for dc in range(2) if dz or dc]
    peers += [device(x, y + 1, z, core), device(x, y + 7, z, core)]
    peers += [device(x + 1, y, z, core), device(x + 3, y, z, core)]
    for peer in peers:
        pl.semaphore_signal(barrier, inc=1, device_id=peer, device_id_type=MESH)

    loads = [
        pltpu.make_async_copy(src, dst, load_sem.at[i])
        for i, (src, dst) in enumerate(
            ((codes_hbm, codes), (exponents_hbm, exponents), (upstream_hbm, upstream)))
    ]
    for copy in loads:
        copy.start()

    def token_columns(q, to_part):
        return pl.ds(pl.multiple_of(q * 2048 + to_part * 640, 128), WINDOW)

    own_copies = [
        pltpu.make_async_copy(
            tokens.at[:, token_columns(q, j)],
            tok.at[rows_of(j), pl.ds(q * WINDOW, WINDOW)],
            tok_own_sem.at[q],
        )
        for q in range(4)
    ]
    for copy in own_copies:
        copy.start()

    packed[...] = jnp.zeros_like(packed)
    loads[0].wait()
    loads[1].wait()
    scale = jnp.exp2(exponents[...].astype(F32)).astype(BF16).astype(F32)
    blank = jnp.zeros((16, 128), BF16)
    for q in range(4):
        for i in range(16):
            b = q * 16 + i
            value = codes[:, b * 128:(b + 1) * 128].astype(F32) * scale[:, b:b + 1]
            to = min(i // 5, 2)
            at = q * 6 + i - 5 * to
            windows[to, :, at * 128:(at + 1) * 128] = value[0:16].astype(BF16)
            run, lane = 3 * (at // 5), at % 5 * 128
            packed[to, run:run + 3, lane:lane + 128] = value[16:19]
        for to in range(2):
            windows[to, :, q * WINDOW + 640:(q + 1) * WINDOW] = blank
    for to in range(3):
        windows[to, :, WIDTH:] = packed[to].astype(BF16)
    mine = pl.ds(pl.multiple_of(16 * j, 16), 16)
    gathered[mine, :] = windows[j]

    pl.semaphore_wait(barrier, len(peers))

    a2a = [
        launch(remote(
            windows.at[part(m)], gathered.at[mine], a2a_s.at[m - 1], a2a_r.at[m - 1], group_peer(m)))
        for m in (1, 2)
    ]

    def unit_rows(u, slot):
        return pl.ds(pl.multiple_of(slot * SLOT + 16 * part(u), 16), 16)

    def ring(u, way, k):
        sign = 1 if way == 0 else -1
        return remote(
            gathered.at[unit_rows(u, slot_of(sign * (k - 1)))],
            gathered.at[unit_rows(u, slot_of(sign * k))],
            ring_s.at[u, way, k - 1], ring_r.at[u, way, k - 1], device(x, y + sign, z, core))

    def ring_last(u):
        odd = lax.rem(core + u, 2)
        return remote(
            gathered.at[unit_rows(u, slot_of(3) + odd)], gathered.at[unit_rows(u, slot_of(4))],
            ring_s.at[u, 0, 3], ring_r.at[u, 0, 3], device(x, y + 1 - 2 * odd, z, core))

    def ring_open(u):
        for way in (0, 1):
            launch(ring(u, way, 1))

    def ring_arrive(u, k):
        if k == 4:
            ring_last(u).wait_recv()
            return
        for way in (0, 1):
            ring(u, way, k).wait_recv()
            if k < 3:
                launch(ring(u, way, k + 1))
        if k == 3:
            launch(ring_last(u))

    ring_open(0)

    at = lax.broadcasted_iota(jnp.int32, (512, 456), 0)
    natural = lax.broadcasted_iota(jnp.int32, (512, 456), 1)
    slot, within = at >> 6, at & 63
    offset = jnp.where((slot & 1) == 1, (slot + 1) >> 1, -(slot >> 1))
    source_y = (y - offset + 8) & 7
    late = within - 48
    late_z = (late >= 3).astype(jnp.int32) + (late >= 6).astype(jnp.int32)
    source_z = jnp.where(late < 0, within >> 4, late_z)
    source_row = jnp.where(late < 0, within & 15, 16 + late - 3 * late_z)
    matches = (natural == (source_z * 8 + source_y) * 19 + source_row) & (late < 9)
    perm[...] = jnp.where(matches, 1.0, 0.0).astype(BF16)
    loads[2].wait()
    up_perm[...] = lax.dot_general(upstream[...], perm[...], NT, preferred_element_type=F32)

    to_row = lax.broadcasted_iota(jnp.int32, (80, 48), 0)
    from_row = lax.broadcasted_iota(jnp.int32, (80, 48), 1)
    run, within = to_row >> 4, to_row & 15
    late_z = (within >= 3).astype(jnp.int32) + (within >= 6).astype(jnp.int32)
    matches = (from_row == 16 * late_z + 3 * run + within - 3 * late_z) & (within < 9)
    unpacker = jnp.where(matches, 1.0, 0.0).astype(BF16)

    def unpack(offset):
        top = slot_of(offset) * SLOT
        rows = jnp.dot(unpacker, gathered[top:top + 48, WIDTH:], preferred_element_type=F32).astype(BF16)
        for c in range(5):
            width = min(PACK, WIDTH - c * PACK)
            gathered[top + 48:top + 64, c * PACK:c * PACK + width] = rows[16 * c:16 * c + 16, :width]

    token_copies = []
    for way, step, to_part in ((0, 1, part(1)), (1, 11, part(2))):
        for q in range(4):
            token_copies.append(remote(
                tokens.at[pl.ds(pl.multiple_of(96 * core, 16), 96), token_columns(q, to_part)],
                tok.at[rows_of(j, 96, 96 * core), pl.ds(q * WINDOW, WINDOW)],
                tok_s.at[way, q], tok_r.at[way, q], device(x, y, z + step, core)))

    def project(c, rows):
        start, width = CHUNKS[c]
        p_part[rows, pl.ds(start, width)] = lax.dot_general(
            tok[rows, :], gathered[start:start + width, :WIDTH], NT, preferred_element_type=F32)

    def offer(c):
        columns = pl.ds(*CHUNKS[c])
        for m in (1, 2):
            p_send[m - 1, :, columns] = p_part[rows_of(part(m)), columns].astype(BF16)
            p_copies[c, m] = launch(remote(
                p_send.at[m - 1, :, columns], p_recv.at[m - 1, :, columns],
                p_s.at[c, m - 1], p_r.at[c, m - 1], group_peer(m)))

    def activate(c):
        columns = pl.ds(*CHUNKS[c])
        for m in (1, 2):
            p_copies[c, m].wait_recv()
        projected = p_part[rows_of(j), columns] + p_recv[0, :, columns].astype(F32) + p_recv[1, :, columns].astype(F32)
        sig = 1.0 / (1.0 + jnp.exp(-projected))
        slope = sig * (1.0 + projected * (1.0 - sig))
        hidden[rows_of(j), columns] = (up_perm[:, columns] * slope).astype(BF16)
        block = hidden.at[rows_of(j), columns]
        for m in (1, 2):
            h_copies.append(launch(remote(
                block, block, h_s.at[c, m - 1], h_r.at[c, m - 1], group_peer(m))))
        act_perm[:, columns] = (projected * sig).astype(BF16)

    p_copies, h_copies = {}, []

    ring_arrive(0, 1)
    for u in (1, 2):
        a2a[2 - u].wait_recv()
        ring_open(u)
    for copy in token_copies:
        launch(copy)
    unpack(0)
    ring_arrive(0, 2)
    ring_arrive(1, 1)
    ring_arrive(2, 1)
    unpack(1)
    unpack(-1)
    ring_arrive(0, 3)
    ring_arrive(1, 2)
    ring_arrive(2, 2)
    unpack(2)
    unpack(-2)
    for copy in own_copies:
        copy.wait()
    project(0, rows_of(j))

    core_copies = []
    for way in (0, 1):
        for q in range(4):
            token_copies[way * 4 + q].wait_recv()
        block = tok.at[rows_of(part(2 - way), 96, 96 * core)]
        core_copies.append(launch(remote(block, block, tokc_s.at[way], tokc_r.at[way], other_core)))

    ring_arrive(0, 4)
    ring_arrive(1, 3)
    for copy in core_copies:
        copy.wait_recv()
    project(0, rows_of(part(1)))
    project(0, rows_of(part(2)))
    offer(0)
    ring_arrive(2, 3)
    unpack(3)
    unpack(-3)
    project(1, slice(None))
    offer(1)
    activate(0)
    ring_arrive(1, 4)
    ring_arrive(2, 4)
    unpack(4)
    project(2, slice(None))
    offer(2)
    activate(1)
    activate(2)
    act_out[...] = jnp.dot(act_perm[...], perm[...], preferred_element_type=F32).astype(BF16)
    for copy in h_copies:
        copy.wait_recv()

    quarters = [lax.rem(x + 2, 4), lax.rem(x + 1, 4), lax.rem(x + 3, 4), x]
    g_copies = []

    def half(i, rows, which):
        columns = pl.ds(pl.multiple_of(quarters[i] * WINDOW + 384 * which, 128), 384)
        return jnp.dot(hidden[rows, :], gathered[:, columns], preferred_element_type=F32)

    def give(i, rows):
        g_send[i, rows, :] = half(i, rows, 1 - core).astype(BF16)
        n = len(g_copies)
        g_copies.append(launch(remote(
            g_send.at[i, rows], g_recv.at[i, rows], g_s.at[n], g_r.at[n], other_core)))

    def keep(i):
        g_own[i] = half(i, pl.ds(0, 3 * ROWS), core)

    def pair_sum(i, rows):
        return g_own[i, rows, :] + g_recv[i, rows, :].astype(F32)

    pieces = 3 * ROWS // PIECE
    sides = (x + 1, x + 3)
    far_copies, near_copies, mid_copies = {}, {}, {}

    def rows_at(p, part_of=None):
        if part_of is None:
            return pl.ds(p * PIECE, PIECE)
        return pl.ds(p * PIECE + part_of * (PIECE // 2), PIECE // 2)

    def send_far(p):
        x_far[rows_at(p), :] = pair_sum(0, rows_at(p)).astype(BF16)
        for way in (0, 1):
            far_copies[p, way] = launch(remote(
                x_far.at[rows_at(p, way)], x_mid.at[rows_at(p, way)],
                m_s.at[p, way], m_r.at[p, way], device(sides[way], y, z, core)))

    def send_near(p):
        for way in (0, 1):
            rows = rows_at(p, 1 - way)
            x_send[way, rows, :] = pair_sum(1 + way, rows).astype(BF16)
            near_copies[p, way] = launch(remote(
                x_send.at[way, rows], x_recv.at[way, rows],
                n_s.at[p, way], n_r.at[p, way], device(sides[way], y, z, core)))

    def send_mid(p):
        for way in (0, 1):
            rows = rows_at(p, way)
            far_copies[p, way].wait_recv()
            x_send[way, rows, :] = (pair_sum(1 + way, rows) + x_mid[rows, :].astype(F32)).astype(BF16)
            mid_copies[p, way] = launch(remote(
                x_send.at[way, rows], x_recv.at[way, rows],
                x_s.at[p, way], x_r.at[p, way], device(sides[way], y, z, core)))

    leaving = []

    def send_owner(p):
        for way in (0, 1):
            near_copies[p, way].wait_recv()
            mid_copies[p, way].wait_recv()
        rows = rows_at(p)
        z_send[rows, :] = (
            pair_sum(3, rows) + x_recv[0, rows, :].astype(F32) + x_recv[1, rows, :].astype(F32)
        ).astype(BF16)
        s, there = p * PIECE // ROWS, p * PIECE % ROWS
        for i in range(3):
            block = 5 * j + 3 * core + i
            owner, side = block // 2, lax.rem(block, 2)
            valid = jnp.logical_or(core == 0, j == 2) if i == 2 else True
            here = jnp.logical_and(owner == z_hi * 2 + core, j == s)
            src = z_send.at[rows, pl.ds(128 * i, 128)]
            dst = z_recv.at[z_hi, pl.ds(there, PIECE), pl.ds(pl.multiple_of(128 * side, 128), 128)]
            arrived = f_r.at[z_hi, side, there // PIECE]
            away = remote(
                src, dst, f_s.at[p, i], arrived, {"inter": x * 8 + owner, "intra": s * 8 + y})
            stay = pltpu.make_async_copy(src, dst, arrived)
            leaves = jnp.logical_and(valid, jnp.logical_not(here))

            @pl.when(leaves)
            def _():
                away.start()

            @pl.when(jnp.logical_and(valid, here))
            def _():
                stay.start()

            leaving.append((leaves, away))

    every = pl.ds(0, 3 * ROWS)
    give(0, pl.ds(0, 288))
    give(0, pl.ds(288, 288))
    keep(0)
    give(1, every)
    give(2, every)
    g_copies[0].wait_recv()
    send_far(0)
    send_far(1)
    keep(1)
    keep(2)
    g_copies[1].wait_recv()
    g_copies[2].wait_recv()
    g_copies[3].wait_recv()
    send_near(0)
    send_near(1)
    give(3, every)
    send_mid(0)
    send_mid(1)
    send_far(2)
    send_far(3)
    send_near(2)
    keep(3)
    g_copies[4].wait_recv()
    send_owner(0)
    send_near(3)
    send_mid(2)
    send_owner(1)
    send_mid(3)
    send_far(4)
    send_far(5)
    send_near(4)
    send_owner(2)
    send_near(5)
    send_mid(4)
    send_owner(3)
    send_mid(5)
    send_owner(4)
    send_owner(5)

    for copy in pending:
        copy.wait_send()
    for leaves, copy in leaving:
        @pl.when(leaves)
        def _():
            copy.wait_send()

    total = None
    for source in range(4):
        for side in range(2):
            for part_of in range(ROWS // PIECE):
                piece = z_recv.at[source, pl.ds(PIECE * part_of, PIECE), pl.ds(128 * side, 128)]
                pltpu.make_async_copy(piece, piece, f_r.at[source, side, part_of]).wait()
        value = z_recv[source].astype(F32)
        total = value if total is None else total + value
    grad_out[...] = total


def per_device(tokens, weight_codes, exponents, upstream):
    vmem = pl.BlockSpec(memory_space=pltpu.VMEM)
    hbm = pl.BlockSpec(memory_space=pltpu.HBM)
    dma = pltpu.SemaphoreType.DMA
    pieces = 3 * ROWS // PIECE
    return pl.pallas_call(
        kernel,
        out_shape=(
            jax.ShapeDtypeStruct((ROWS, 456), BF16),
            jax.ShapeDtypeStruct((ROWS, 256), F32),
        ),
        in_specs=[hbm] * 4,
        out_specs=(vmem, vmem),
        scratch_shapes=[
            pltpu.VMEM((19, 8192), BF16),
            pltpu.VMEM((19, 64), jnp.int32),
            pltpu.VMEM((ROWS, 456), BF16),
            pltpu.VMEM((3, 16, UNIT), BF16),
            pltpu.VMEM((3, 16, PACK), F32),
            pltpu.VMEM((512, UNIT), BF16),
            pltpu.VMEM((3 * ROWS, WIDTH), BF16),
            pltpu.VMEM((512, 456), BF16),
            pltpu.VMEM((ROWS, 512), F32),
            pltpu.VMEM((3 * ROWS, 512), F32),
            pltpu.VMEM((2, ROWS, 512), BF16),
            pltpu.VMEM((2, ROWS, 512), BF16),
            pltpu.VMEM((ROWS, 512), BF16),
            pltpu.VMEM((3 * ROWS, 512), BF16),
            pltpu.VMEM((4, 3 * ROWS, 384), BF16),
            pltpu.VMEM((4, 3 * ROWS, 384), BF16),
            pltpu.VMEM((4, 3 * ROWS, 384), F32),
            pltpu.VMEM((3 * ROWS, 384), BF16),
            pltpu.VMEM((2, 3 * ROWS, 384), BF16),
            pltpu.VMEM((3 * ROWS, 384), BF16),
            pltpu.VMEM((2, 3 * ROWS, 384), BF16),
            pltpu.VMEM((3 * ROWS, 384), BF16),
            pltpu.VMEM((4, ROWS, 256), BF16),
            dma((3,)), dma((4,)),
            dma((2,)), dma((2,)),
            dma((3, 2, 4)), dma((3, 2, 4)),
            dma((2, 4)), dma((2, 4)),
            dma((2,)), dma((2,)),
            dma((3, 2)), dma((3, 2)),
            dma((3, 2)), dma((3, 2)),
            dma((5,)), dma((5,)),
            dma((pieces, 2)), dma((pieces, 2)),
            dma((pieces, 2)), dma((pieces, 2)),
            dma((pieces, 2)), dma((pieces, 2)),
            dma((pieces, 3)), dma((4, 2, ROWS // PIECE)),
        ],
        compiler_params=pltpu.CompilerParams(
            collective_id=0, has_side_effects=True, vmem_limit_bytes=48 << 20),
        cost_estimate=pl.CostEstimate(
            flops=4 * ROWS * 8192 * 456, bytes_accessed=8 << 20, transcendentals=ROWS * 512),
    )(tokens, weight_codes, exponents, upstream)


def solution(mesh):
    placed = (
        P("intra", None),
        P(("inter", "intra"), None),
        P(("inter", "intra"), None),
        P("intra", "inter"),
    )
    return jax.shard_map(
        per_device,
        mesh=mesh,
        in_specs=placed,
        out_specs=(P("intra", "inter"), P("intra", "inter")),
        check_vma=False,
    )
```

time: 112 us -> 102 us (0.911)
  Pallas kernels: 105 us -> 95.5 us
    pallas_call x1, Pallas kernels: 105 us -> 95.5 us  [per_device(): pl.pallas_call(kernel, out_shape=(jax.ShapeDtypeStruct((ROWS, 456), BF16)...]
where the time goes in v2:
time: 102 us
  Pallas kernels  95.5 us (94%)
  local copies, waits for them, and re-layouts  5.87 us (6%)
    pallas_call x1, Pallas kernels, per_device(): pl.pallas_call(kernel, out_shape=(jax.ShapeDtypeStruct((ROWS, 456), BF16)...  95.5 us
    unnamed x10, local copies, waits for them, and re-layouts  5.87 us

profile of v2, /device:TPU:129, one launch (start us, length us, event | category | flops | bytes accessed | tf_op | source)
XLA Modules:
  0.0 102.1 jit_solution(9207576169447972081)
XLA Ops:
  0.6 0.0 copy-start
  0.6 1.9 %copy-done = bf16[192,8192]{1,0:T(8,128)(2,1)S(1)} copy-done((bf16[192,8192]{1,0:T(8,128)(2,1)S(1)}, bf16[192,8192]{1,0:T(8,128)(2,1)}, u32[]{:S(2)}) %copy-start) | copy-done | bytes 3145752
  2.5 0.0 copy-start.1
  2.5 1.0 copy-done.1
  3.5 0.0 copy-start.2
  3.5 0.9 copy-done.2
  4.4 0.0 copy-start.3
  4.4 0.7 copy-done.3
  5.2 95.5 %shard_map.59 = (bf16[192,456]{1,0:T(8,128)(2,1)S(1)}, f32[192,256]{1,0:T(8,128)S(1)}) custom-call(bf16[192,8192]{1,0:T(8,128)(2,1)S(1)} %copy-done, bf16[19,8192]{1,0:T(8,128)(2,1)S(1)} %copy-done.1, s32[19,64]{1,0:T(8,128)S(1)} %copy-done.3, bf16[192,456]{1,0:T(8,128)(2,1)S(1)} %copy-done.2), custom_call_target="tpu_custom_call" | custom-call | flops 2868903936 | bytes 8388608 | tf_op jit(solution)/shard_map/pallas_call | solution.py:428
  100.7 0.7 copy.8
  101.4 0.7 copy.9
Async XLA Ops:
  0.6 1.9 %copy-start = (bf16[192,8192]{1,0:T(8,128)(2,1)S(1)}, bf16[192,8192]{1,0:T(8,128)(2,1)}, u32[]{:S(2)}) copy-start(bf16[192,8192]{1,0:T(8,128)(2,1)} %tokens.1) | copy-start | bytes 9437188
  2.5 1.0 copy-start.1
  3.5 0.9 copy-start.2
  4.4 0.7 copy-start.3

commit v3 on v2

--- a/solution.py
+++ b/solution.py
@@ -15,6 +15,7 @@
 SLOT = 64
 PACK = 640
 UNIT = WIDTH + PACK
+AHEAD = 2
 PIECE = 96
 CHUNKS = ((0, 256), (256, 128), (384, 128))
 NT = (((1,), (1,)), ((), ()))
@@ -36,7 +37,7 @@
     codes, exponents, upstream,
     windows, packed, gathered, tok, perm, up_perm, p_part, p_send, p_recv, act_perm, hidden,
     g_send, g_recv, g_own, x_far, x_send, x_mid, x_recv, z_send, z_recv,
-    load_sem, tok_own_sem, a2a_s, a2a_r, ring_s, ring_r, tok_s, tok_r, tokc_s, tokc_r,
+    load_sem, tok_own_sem, a2a_s, a2a_r, ring_s, ring_r, tok_s, tok_r, tokx_s, tokx_r, tokc_s, tokc_r,
     p_s, p_r, h_s, h_r, g_s, g_r, m_s, m_r, n_s, n_r, x_s, x_r, f_s, f_r,
 ):
     inter = lax.axis_index("inter")
@@ -142,9 +143,18 @@
             gathered.at[unit_rows(u, slot_of(3) + odd)], gathered.at[unit_rows(u, slot_of(4))],
             ring_s.at[u, 0, 3], ring_r.at[u, 0, 3], device(x, y + 1 - 2 * odd, z, core))
 
+    leaving_to = ([], [])
+
+    def ring_launch(copy, ways):
+        for way in ways:
+            if len(leaving_to[way]) >= AHEAD:
+                leaving_to[way].pop(0).wait_send()
+            leaving_to[way].append(copy)
+        copy.start()
+
     def ring_open(u):
         for way in (0, 1):
-            launch(ring(u, way, 1))
+            ring_launch(ring(u, way, 1), (way,))
 
     def ring_arrive(u, k):
         if k == 4:
@@ -153,7 +163,7 @@
         for way in (0, 1):
             ring(u, way, k).wait_recv()
             if k < 3:
-                launch(ring(u, way, k + 1))
+                ring_launch(ring(u, way, k + 1), (way,))
         if k == 3:
             launch(ring_last(u))
 
@@ -187,13 +197,29 @@
             width = min(PACK, WIDTH - c * PACK)
             gathered[top + 48:top + 64, c * PACK:c * PACK + width] = rows[16 * c:16 * c + 16, :width]
 
-    token_copies = []
-    for way, step, to_part in ((0, 1, part(1)), (1, 11, part(2))):
-        for q in range(4):
-            token_copies.append(remote(
-                tokens.at[pl.ds(pl.multiple_of(96 * core, 16), 96), token_columns(q, to_part)],
-                tok.at[rows_of(j, 96, 96 * core), pl.ds(q * WINDOW, WINDOW)],
+    quarter = 96 * core + 48 * lax.rem(x, 2)
+    token_copies, side_copies, core_copies = {}, {}, {}
+
+    def tokens_ask(q):
+        for way, step, to_part in ((0, 1, part(1)), (1, 11, part(2))):
+            token_copies[way, q] = launch(remote(
+                tokens.at[pl.ds(pl.multiple_of(quarter, 16), 48), token_columns(q, to_part)],
+                tok.at[rows_of(j, 48, quarter), pl.ds(q * WINDOW, WINDOW)],
                 tok_s.at[way, q], tok_r.at[way, q], device(x, y, z + step, core)))
+
+    def tokens_aside(q):
+        for way, step in ((0, 1), (1, 3)):
+            token_copies[way, q].wait_recv()
+            block = tok.at[rows_of(part(2 - way), 48, quarter), pl.ds(q * WINDOW, WINDOW)]
+            side_copies[way, q] = launch(remote(
+                block, block, tokx_s.at[way, q], tokx_r.at[way, q], device(x + step, y, z, core)))
+
+    def tokens_across(q):
+        for way in (0, 1):
+            side_copies[way, q].wait_recv()
+            block = tok.at[rows_of(part(2 - way), 96, 96 * core), pl.ds(q * WINDOW, WINDOW)]
+            core_copies[way, q] = launch(remote(
+                block, block, tokc_s.at[way, q], tokc_r.at[way, q], other_core))
 
     def project(c, rows):
         start, width = CHUNKS[c]
@@ -228,37 +254,37 @@
     for u in (1, 2):
         a2a[2 - u].wait_recv()
         ring_open(u)
-    for copy in token_copies:
-        launch(copy)
+    for q in range(4):
+        tokens_ask(q)
     unpack(0)
     ring_arrive(0, 2)
+    tokens_aside(0)
     ring_arrive(1, 1)
+    tokens_aside(1)
     ring_arrive(2, 1)
+    tokens_aside(2)
     unpack(1)
     unpack(-1)
+    tokens_aside(3)
+    tokens_across(0)
     ring_arrive(0, 3)
+    tokens_across(1)
+    tokens_across(2)
     ring_arrive(1, 2)
+    tokens_across(3)
     ring_arrive(2, 2)
     unpack(2)
     unpack(-2)
     for copy in own_copies:
         copy.wait()
     project(0, rows_of(j))
-
-    core_copies = []
-    for way in (0, 1):
-        for q in range(4):
-            token_copies[way * 4 + q].wait_recv()
-        block = tok.at[rows_of(part(2 - way), 96, 96 * core)]
-        core_copies.append(launch(remote(block, block, tokc_s.at[way], tokc_r.at[way], other_core)))
-
     ring_arrive(0, 4)
-    ring_arrive(1, 3)
-    for copy in core_copies:
+    for copy in core_copies.values():
         copy.wait_recv()
     project(0, rows_of(part(1)))
     project(0, rows_of(part(2)))
     offer(0)
+    ring_arrive(1, 3)
     ring_arrive(2, 3)
     unpack(3)
     unpack(-3)
@@ -402,7 +428,7 @@
     send_owner(4)
     send_owner(5)
 
-    for copy in pending:
+    for copy in pending + leaving_to[0] + leaving_to[1]:
         copy.wait_send()
     for leaves, copy in leaving:
         @pl.when(leaves)
@@ -461,7 +487,8 @@
             dma((2,)), dma((2,)),
             dma((3, 2, 4)), dma((3, 2, 4)),
             dma((2, 4)), dma((2, 4)),
-            dma((2,)), dma((2,)),
+            dma((2, 4)), dma((2, 4)),
+            dma((2, 4)), dma((2, 4)),
             dma((3, 2)), dma((3, 2)),
             dma((3, 2)), dma((3, 2)),
             dma((5,)), dma((5,)),
@@ -471,7 +498,7 @@
             dma((pieces, 3)), dma((4, 2, ROWS // PIECE)),
         ],
         compiler_params=pltpu.CompilerParams(
-            collective_id=0, has_side_effects=True, vmem_limit_bytes=48 << 20),
+            collective_id=0, has_side_effects=True, vmem_limit_bytes=107 << 19),
         cost_estimate=pl.CostEstimate(
             flops=4 * ROWS * 8192 * 456, bytes_accessed=8 << 20, transcendentals=ROWS * 512),
     )(tokens, weight_codes, exponents, upstream)

time: 102 us -> 96.5 us (0.946)
  local copies, waits for them, and re-layouts: 5.87 us -> 2.06 us
  Pallas kernels: 95.5 us -> 93.6 us
    unnamed x10 -> x4, local copies, waits for them, and re-layouts: 5.87 us -> 2.06 us
    pallas_call x1, Pallas kernels: 95.5 us -> 93.6 us  [per_device(): pl.pallas_call(kernel, out_shape=(jax.ShapeDtypeStruct((ROWS, 456), BF16)...]
where the time goes in v3:
time: 96.5 us; the launch traced here: 96.3 us
  Pallas kernels  93.6 us (97%)
  local copies, waits for them, and re-layouts  2.06 us (2%)
    pallas_call x1, Pallas kernels, per_device(): pl.pallas_call(kernel, out_shape=(jax.ShapeDtypeStruct((ROWS, 456), BF16)...  93.6 us
    unnamed x4, local copies, waits for them, and re-layouts  2.06 us

profile of v3, /device:TPU:129, one launch (start us, length us, event | category | flops | bytes accessed | tf_op | source)
XLA Modules:
  0.0 96.3 jit_solution(7123296861053347760)
XLA Ops:
  0.6 0.0 copy-start
  0.6 0.7 copy-done
  1.3 93.6 %shard_map.59 = (bf16[192,456]{1,0:T(8,128)(2,1)S(1)}, f32[192,256]{1,0:T(8,128)S(1)}) custom-call(bf16[192,8192]{1,0:T(8,128)(2,1)} %tokens.1, bf16[19,8192]{1,0:T(8,128)(2,1)} %codes_hbm.1, s32[19,64]{1,0:T(8,128)S(1)} %copy-done, bf16[192,456]{1,0:T(8,128)(2,1)} %upstream_hbm.1), custom_call_target="tpu_custom_call" | custom-call | flops 2868903936 | bytes 8388608 | tf_op jit(solution)/shard_map/pallas_call | solution.py:454
  94.9 0.7 copy.8
  95.6 0.7 copy.9
Async XLA Ops:
  0.6 0.7 copy-start

commit v4 on v3

--- a/solution.py
+++ b/solution.py
@@ -37,7 +37,7 @@
     codes, exponents, upstream,
     windows, packed, gathered, tok, perm, up_perm, p_part, p_send, p_recv, act_perm, hidden,
     g_send, g_recv, g_own, x_far, x_send, x_mid, x_recv, z_send, z_recv,
-    load_sem, tok_own_sem, a2a_s, a2a_r, ring_s, ring_r, tok_s, tok_r, tokx_s, tokx_r, tokc_s, tokc_r,
+    end_sem, round_sem, load_sem, tok_own_sem, a2a_s, a2a_r, ring_s, ring_r, tok_s, tok_r, tokx_s, tokx_r, tokc_s, tokc_r,
     p_s, p_r, h_s, h_r, g_s, g_r, m_s, m_r, n_s, n_r, x_s, x_r, f_s, f_r,
 ):
     inter = lax.axis_index("inter")
@@ -69,13 +69,6 @@
         pending.append(copy)
         return copy
 
-    barrier = pltpu.get_barrier_semaphore()
-    peers = [device(x, y, z + dz, core + dc) for dz in range(12) for dc in range(2) if dz or dc]
-    peers += [device(x, y + 1, z, core), device(x, y + 7, z, core)]
-    peers += [device(x + 1, y, z, core), device(x + 3, y, z, core)]
-    for peer in peers:
-        pl.semaphore_signal(barrier, inc=1, device_id=peer, device_id_type=MESH)
-
     loads = [
         pltpu.make_async_copy(src, dst, load_sem.at[i])
         for i, (src, dst) in enumerate(
@@ -83,6 +76,23 @@
     ]
     for copy in loads:
         copy.start()
+
+    barrier = pltpu.get_barrier_semaphore()
+    peers = [other_core, group_peer(1), group_peer(2)]
+    peers += [device(x, y + 1, z, core), device(x, y + 7, z, core)]
+    peers += [device(x + 1, y, z, core), device(x + 3, y, z, core)]
+    below = [device(x, y, z + 11, core), device(x, y, z + 11, core + 1)]
+    above = [device(x, y, z + 1, core), device(x, y, z + 1, core + 1)]
+
+    def greet(semaphore, devices):
+        for peer in devices:
+            pl.semaphore_signal(semaphore, inc=1, device_id=peer, device_id_type=MESH)
+
+    greet(barrier, peers + below)
+
+    @pl.when(z != 11)
+    def _():
+        greet(barrier, above)
 
     def token_columns(q, to_part):
         return pl.ds(pl.multiple_of(q * 2048 + to_part * 640, 128), WINDOW)
@@ -119,7 +129,11 @@
     mine = pl.ds(pl.multiple_of(16 * j, 16), 16)
     gathered[mine, :] = windows[j]
 
-    pl.semaphore_wait(barrier, len(peers))
+    pl.semaphore_wait(barrier, jnp.where(z == 0, len(peers) + 2, len(peers) + 4))
+
+    @pl.when(z == 11)
+    def _():
+        greet(end_sem, above)
 
     a2a = [
         launch(remote(
@@ -200,12 +214,32 @@
     quarter = 96 * core + 48 * lax.rem(x, 2)
     token_copies, side_copies, core_copies = {}, {}, {}
 
-    def tokens_ask(q):
-        for way, step, to_part in ((0, 1, part(1)), (1, 11, part(2))):
-            token_copies[way, q] = launch(remote(
-                tokens.at[pl.ds(pl.multiple_of(quarter, 16), 48), token_columns(q, to_part)],
-                tok.at[rows_of(j, 48, quarter), pl.ds(q * WINDOW, WINDOW)],
-                tok_s.at[way, q], tok_r.at[way, q], device(x, y, z + step, core)))
+    def tokens_to(way, q, to, semaphores):
+        return remote(
+            tokens.at[
+                pl.ds(pl.multiple_of(quarter, 16), 48), token_columns(q, part(1 + way))],
+            tok.at[rows_of(j, 48, quarter), pl.ds(q * WINDOW, WINDOW)],
+            semaphores.at[q], tok_r.at[way, q], to)
+
+    token_again = []
+    for q in range(4):
+        token_copies[0, q] = tokens_to(0, q, device(x, y, z + 1, core), tok_s.at[0])
+        token_copies[1, q] = tokens_to(1, q, device(x, y, z + 11, core), tok_s.at[1])
+        token_again.append(tokens_to(0, q, device(x, y, z + 10, core), tok_s.at[2]))
+    token_sends = (
+        (z != 11, [token_copies[0, q] for q in range(4)]),
+        (z == 2, token_again),
+        (z != 0, [token_copies[1, q] for q in range(4)]),
+        (z == 0, [token_copies[1, q] for q in range(4)]),
+    )
+
+    def tokens_send(n):
+        condition, copies = token_sends[n]
+
+        @pl.when(condition)
+        def _():
+            for copy in copies:
+                copy.start()
 
     def tokens_aside(q):
         for way, step in ((0, 1), (1, 3)):
@@ -254,14 +288,28 @@
     for u in (1, 2):
         a2a[2 - u].wait_recv()
         ring_open(u)
-    for q in range(4):
-        tokens_ask(q)
+    def tell(n):
+        step = 1 if n == 0 else 2
+        greet(round_sem.at[n], [device(x, y, z + step, core), device(x, y, z + 12 - step, core)])
+
+    def hear(n):
+        pl.semaphore_wait(round_sem.at[n], 2)
+
+    for n in (0, 2, 1):
+        tokens_send(n)
     unpack(0)
     ring_arrive(0, 2)
     tokens_aside(0)
     ring_arrive(1, 1)
     tokens_aside(1)
     ring_arrive(2, 1)
+
+    @pl.when(z == 0)
+    def _():
+        pl.semaphore_wait(end_sem, 2)
+
+    tokens_send(3)
+    tell(0)
     tokens_aside(2)
     unpack(1)
     unpack(-1)
@@ -286,6 +334,8 @@
     offer(0)
     ring_arrive(1, 3)
     ring_arrive(2, 3)
+    hear(0)
+    tell(1)
     unpack(3)
     unpack(-3)
     project(1, slice(None))
@@ -293,6 +343,8 @@
     activate(0)
     ring_arrive(1, 4)
     ring_arrive(2, 4)
+    hear(1)
+    tell(2)
     unpack(4)
     project(2, slice(None))
     offer(2)
@@ -412,6 +464,7 @@
     send_near(2)
     keep(3)
     g_copies[4].wait_recv()
+    hear(2)
     send_owner(0)
     send_near(3)
     send_mid(2)
@@ -430,6 +483,11 @@
 
     for copy in pending + leaving_to[0] + leaving_to[1]:
         copy.wait_send()
+    for condition, copies in token_sends:
+        @pl.when(condition)
+        def _():
+            for copy in copies:
+                copy.wait_send()
     for leaves, copy in leaving:
         @pl.when(leaves)
         def _():
@@ -483,10 +541,11 @@
             pltpu.VMEM((2, 3 * ROWS, 384), BF16),
             pltpu.VMEM((3 * ROWS, 384), BF16),
             pltpu.VMEM((4, ROWS, 256), BF16),
+            pltpu.SemaphoreType.REGULAR, pltpu.SemaphoreType.REGULAR((3,)),
             dma((3,)), dma((4,)),
             dma((2,)), dma((2,)),
             dma((3, 2, 4)), dma((3, 2, 4)),
-            dma((2, 4)), dma((2, 4)),
+            dma((3, 4)), dma((2, 4)),
             dma((2, 4)), dma((2, 4)),
             dma((2, 4)), dma((2, 4)),
             dma((3, 2)), dma((3, 2)),

time: 96.5 us -> 94.1 us (0.975)
  Pallas kernels: 93.6 us -> 91.2 us
    pallas_call x1, Pallas kernels: 93.6 us -> 91.2 us  [per_device(): pl.pallas_call(kernel, out_shape=(jax.ShapeDtypeStruct((ROWS, 456), BF16)...]
where the time goes in v4:
time: 94.1 us; the launch traced here: 93.9 us
  Pallas kernels  91.2 us (97%)
  local copies, waits for them, and re-layouts  2.06 us (2%)
    pallas_call x1, Pallas kernels, per_device(): pl.pallas_call(kernel, out_shape=(jax.ShapeDtypeStruct((ROWS, 456), BF16)...  91.2 us
    unnamed x4, local copies, waits for them, and re-layouts  2.06 us

profile of v4, /device:TPU:129, one launch (start us, length us, event | category | flops | bytes accessed | tf_op | source)
XLA Modules:
  0.0 93.9 jit_solution(10626449580201091973)
XLA Ops:
  0.6 0.0 copy-start
  0.6 0.7 copy-done
  1.3 91.2 %shard_map.59 = (bf16[192,456]{1,0:T(8,128)(2,1)S(1)}, f32[192,256]{1,0:T(8,128)S(1)}) custom-call(bf16[192,8192]{1,0:T(8,128)(2,1)} %tokens.1, bf16[19,8192]{1,0:T(8,128)(2,1)} %codes_hbm.1, s32[19,64]{1,0:T(8,128)S(1)} %copy-done, bf16[192,456]{1,0:T(8,128)(2,1)} %upstream_hbm.1), custom_call_target="tpu_custom_call" | custom-call | flops 2868903936 | bytes 8388608 | tf_op jit(solution)/shard_map/pallas_call | solution.py:512
  92.5 0.7 copy.8
  93.2 0.7 copy.9
Async XLA Ops:
  0.6 0.7 copy-start

commit v5 on v4

--- a/solution.py
+++ b/solution.py
@@ -441,25 +441,25 @@
             leaving.append((leaves, away))
 
     every = pl.ds(0, 3 * ROWS)
-    give(0, pl.ds(0, 288))
-    give(0, pl.ds(288, 288))
+    give(0, pl.ds(0, ROWS))
+    give(0, pl.ds(ROWS, 2 * ROWS))
     keep(0)
     give(1, every)
-    give(2, every)
     g_copies[0].wait_recv()
     send_far(0)
     send_far(1)
+    give(2, every)
+    g_copies[1].wait_recv()
+    send_far(2)
     keep(1)
     keep(2)
-    g_copies[1].wait_recv()
     g_copies[2].wait_recv()
     g_copies[3].wait_recv()
     send_near(0)
+    send_mid(0)
     send_near(1)
+    send_mid(1)
     give(3, every)
-    send_mid(0)
-    send_mid(1)
-    send_far(2)
     send_far(3)
     send_near(2)
     keep(3)

time: 94.1 us -> 94.3 us (level)
  no operation moved by 1% of the time
where the time goes in v5:
time: 94.3 us; the launch traced here: 94.1 us
  Pallas kernels  91.4 us (97%)
  local copies, waits for them, and re-layouts  2.06 us (2%)
    pallas_call x1, Pallas kernels, per_device(): pl.pallas_call(kernel, out_shape=(jax.ShapeDtypeStruct((ROWS, 456), BF16)...  91.4 us
    unnamed x4, local copies, waits for them, and re-layouts  2.06 us

profile of v5, /device:TPU:129, one launch (start us, length us, event | category | flops | bytes accessed | tf_op | source)
XLA Modules:
  0.0 94.1 jit_solution(4754769346887155034)
XLA Ops:
  0.6 0.0 copy-start
  0.6 0.7 copy-done
  1.3 91.4 %shard_map.59 = (bf16[192,456]{1,0:T(8,128)(2,1)S(1)}, f32[192,256]{1,0:T(8,128)S(1)}) custom-call(bf16[192,8192]{1,0:T(8,128)(2,1)} %tokens.1, bf16[19,8192]{1,0:T(8,128)(2,1)} %codes_hbm.1, s32[19,64]{1,0:T(8,128)S(1)} %copy-done, bf16[192,456]{1,0:T(8,128)(2,1)} %upstream_hbm.1), custom_call_target="tpu_custom_call" | custom-call | flops 2868903936 | bytes 8388608 | tf_op jit(solution)/shard_map/pallas_call | solution.py:512
  92.8 0.7 copy.8
  93.5 0.7 copy.9
Async XLA Ops:
  0.6 0.7 copy-start
